TPU v7x, 32 devices: a whole 2x2x4 slice. The times are simulated.
32 devices in a mesh: groups: 2 (over x), tm: 16 (over z, y, core).
Axes of the slice: x: 2, y: 2, z: 4, core: 2. Of those that a mesh axis runs over, the one named last changes fastest.
Arguments:
- perambulator: bfloat16 [64, 768, 1536], P('groups', 'tm'), parts along dimension 0, may hold values from -6 to 6
- elementals: bfloat16 [32, 16, 192, 384], P(('groups', 'tm')), parts along dimension 0, may hold values from -0.3125 to 0.3125
- diagrams: int32 [32, 3, 2], P('tm'), may hold values from 0 to 15
- counts: int32 [32], P('tm'), may hold values from 1 to 3, as said below
Outputs:
- correlator: float32 [64, 3, 2], P(('groups', 'tm')), parts along dimension 0
There are 2 independent parts, one for each index of `groups`. A program takes and returns all parts, laid end to end along the dimension named above; an argument that names none is the same for every part. Nothing has to cross between parts.
Inputs may be any that keep to these rules, and one draw needn't show every extreme that they name: `counts`: each pair lists 1 to 3 diagrams; in every draw some pair lists exactly 3. `diagrams`: slots at or beyond a pair's count are ignored.
All inputs are finite; a program needn't handle non-finite values.
Results may differ from a plain program's by a relative error of at most 0.0029.
Values may be sent and summed in bfloat16 or wider, within the bound.
No kernel may reach another device: no remote copies, remote signals or barrier semaphores. Data moves between devices by JAX's collectives and lax.ppermute only.
A program may use at most 128 MiB of HBM per device.

v0:
```python
import functools

import jax
import jax.numpy as jnp
from jax import lax
from jax.experimental import pallas as pl
from jax.experimental.pallas import tpu as pltpu
from jax.sharding import PartitionSpec as P

NT_DIMS = (((1,), (1,)), ((), ()))
ANYWHERE = pl.BlockSpec(memory_space=pl.ANY)
VMEM_BYTES = 56 * 1024 * 1024
HBM = pl.BlockSpec(memory_space=pltpu.HBM)
VMEM = pl.BlockSpec(memory_space=pltpu.VMEM)
SMEM = pl.BlockSpec(memory_space=pltpu.SMEM)


def exchanged(x, mask):
    devices = lax.axis_size("tm")
    return lax.ppermute(x, "tm", [(i, i ^ mask) for i in range(devices)])


def passed_along(x, by, mask=0):
    devices = lax.axis_size("tm")
    return lax.ppermute(x, "tm", [(i, ((i + by) % devices) ^ mask) for i in range(devices)])


def regroup_kernel(high_ref, source_ref, out_ref, block_ref, in_sems, out_sems):
    high = high_ref[0]
    copies = []
    for j in range(source_ref.shape[1]):
        for side in range(2):
            which = 1 - high if side == 0 else high
            block = block_ref.at[j, side]
            n = 2 * j + side
            copies.append(
                (
                    pltpu.make_async_copy(source_ref.at[which, j], block, in_sems.at[n]),
                    pltpu.make_async_copy(block, out_ref.at[j, side], out_sems.at[n]),
                )
            )
    for copy_in, _ in copies:
        copy_in.start()
    for copy_in, copy_out in copies:
        copy_in.wait()
        copy_out.start()
    for _, copy_out in copies:
        copy_out.wait()


def regrouped(perambulator, high, half, pair_count):
    columns, width = perambulator.shape[1:]
    source = perambulator.reshape(2, half, pair_count, columns, width)
    shape = (half, 2, pair_count, columns, width)
    return pl.pallas_call(
        regroup_kernel,
        in_specs=[SMEM, HBM],
        out_specs=HBM,
        out_shape=jax.ShapeDtypeStruct(shape, perambulator.dtype),
        scratch_shapes=[
            pltpu.VMEM(shape, perambulator.dtype),
            pltpu.SemaphoreType.DMA((2 * half,)),
            pltpu.SemaphoreType.DMA((2 * half,)),
        ],
        compiler_params=pltpu.CompilerParams(vmem_limit_bytes=58 * 1024 * 1024),
    )(high.reshape(1), source)


def tied(x, *earlier):
    return pl.pallas_call(
        lambda *refs: None,
        in_specs=[ANYWHERE] * (1 + len(earlier)),
        out_specs=ANYWHERE,
        out_shape=jax.ShapeDtypeStruct(x.shape, x.dtype),
        input_output_aliases={0: 0},
    )(x, *earlier)


def halves_swapped(x):
    vectors = x.shape[1] // 2
    return jnp.concatenate([x[:, vectors:], x[:, :vectors]], axis=1)


def pairs_kernel(pairs, lead, first, counts_ref, begin_ref, tau_ref, *refs):
    sink_refs = refs[:pairs]
    source_ref, out_ref, sinks, sources, both_ref, left_ref, sink_sems, source_sems = refs[pairs:]
    slots, vectors, packed = sinks.shape[1:]
    spins, _, width = left_ref.shape
    blocks = width // packed
    pieces = tau_ref.shape[0] // spins
    pair = pl.program_id(0)
    first_half = lax.broadcasted_iota(jnp.int32, (vectors, packed), 1) < vectors

    @pl.when(pair == 0)
    def _():
        for p in range(pairs):
            for d in range(slots):

                @pl.when(d < counts_ref[first + p])
                def _():
                    pltpu.make_async_copy(
                        sink_refs[p].at[d], sinks.at[p, d], sink_sems.at[p, d]
                    ).start()
                    pltpu.make_async_copy(
                        source_ref.at[first + p, d], sources.at[p, d], source_sems.at[p, d]
                    ).start()

        for p in range(out_ref.shape[0]):
            for d in range(slots):
                for side in range(2):
                    out_ref[p, side, d] = begin_ref[p, side, d]

    for s in range(spins):
        for b in range(blocks):
            lanes = slice(b * packed, (b + 1) * packed)
            tile = tau_ref[s * pieces : (s + 1) * pieces, 0, :, lanes].reshape(vectors, packed)
            swapped = halves_swapped(tile)
            both_ref[s, :vectors, lanes] = tile
            both_ref[s, vectors:, lanes] = jnp.where(first_half, -swapped, swapped)

    @pl.loop(0, counts_ref[first + pair])
    def _(d):
        pltpu.make_async_copy(
            sink_refs[0].at[0], sinks.at[pair, d], sink_sems.at[pair, d]
        ).wait()
        sink = sinks[pair, d]
        embedding = jnp.concatenate(
            [jnp.where(first_half, sink, -sink), halves_swapped(sink)], axis=0
        )
        for s in range(spins):
            stacked = jnp.concatenate(
                [both_ref[s, :vectors, b * packed : (b + 1) * packed] for b in range(blocks)],
                axis=0,
            )
            left = lax.dot_general(
                stacked, embedding, NT_DIMS, preferred_element_type=jnp.float32
            ).astype(jnp.bfloat16)
            for b in range(blocks):
                left_ref[s, :, b * packed : (b + 1) * packed] = left[
                    b * vectors : (b + 1) * vectors
                ]
        block = jnp.zeros((2 * vectors, vectors), jnp.float32)
        for s in range(spins):
            block += lax.dot_general(
                both_ref[s], left_ref[s], NT_DIMS, preferred_element_type=jnp.float32
            )
        pltpu.make_async_copy(
            source_ref.at[0, 0], sources.at[pair, d], source_sems.at[pair, d]
        ).wait()
        source = sources[pair, d].astype(jnp.float32).T
        real = source[:vectors]
        imag = source[vectors:]
        block_real = block[:vectors]
        block_imag = block[vectors:]
        row = lead + first + pair
        out_ref[row, 0, d] += jnp.sum(real * block_real - imag * block_imag)
        out_ref[row, 1, d] += jnp.sum(real * block_imag + imag * block_real)


def pairs_sums(tau, side, first, sinks, sources, counts, begin):
    pairs = len(sinks)
    slots, vectors, packed = sinks[0].shape
    pieces, _, columns, width = tau.shape
    spins = pieces * columns // vectors
    lead = side * counts.shape[0]
    flops = 4 * pairs * spins * slots * width * vectors * packed
    moved = 2 * pairs * (spins * vectors * width + 2 * slots * vectors * packed)
    elemental_copies = [pltpu.VMEM((pairs, slots, vectors, packed), jnp.bfloat16)] * 2
    return pl.pallas_call(
        functools.partial(pairs_kernel, pairs, lead, first),
        grid=(pairs,),
        in_specs=[
            SMEM,
            SMEM,
            pl.BlockSpec((pieces, 1, columns, width), lambda p: (0, lead + first + p, 0, 0)),
        ]
        + [HBM] * (pairs + 1),
        out_specs=SMEM,
        out_shape=jax.ShapeDtypeStruct(begin.shape, jnp.float32),
        scratch_shapes=elemental_copies
        + [
            pltpu.VMEM((spins, 2 * vectors, width), jnp.bfloat16),
            pltpu.VMEM((spins, vectors, width), jnp.bfloat16),
            pltpu.SemaphoreType.DMA((pairs, slots)),
            pltpu.SemaphoreType.DMA((pairs, slots)),
        ],
        compiler_params=pltpu.CompilerParams(vmem_limit_bytes=VMEM_BYTES),
        cost_estimate=pl.CostEstimate(flops=flops, bytes_accessed=moved, transcendentals=0),
    )(counts, begin, tau, *sinks, sources)


def body(perambulator, elementals, diagrams, counts):
    devices = lax.axis_size("tm")
    me = lax.axis_index("tm")
    pair_count, slots = diagrams.shape[:2]
    columns, width = perambulator.shape[1:]
    vectors, packed = elementals.shape[2:]
    half = devices // 2
    own_set = elementals[0]
    high = (me >= half).astype(jnp.int32)
    halves = [list(range(half)), list(range(half, devices))]

    steps = [(slot + 1) * devices // (pair_count + 1) for slot in range(pair_count)]
    wanted = [passed_along(diagrams[slot, :, 0], by) for slot, by in enumerate(steps)]
    given_counts = exchanged(counts, half)
    own_sources = jnp.take(own_set, diagrams[:, :, 1].reshape(-1), axis=0, mode="clip")
    own_sources = own_sources.reshape(pair_count, slots, vectors, packed)
    given_sources = exchanged(own_sources, half)
    chosen = [jnp.take(own_set, index, axis=0, mode="clip") for index in wanted]
    given_sinks = [passed_along(sets, -by, half) for by, sets in zip(steps, chosen)]
    last = pair_count - 1
    own_sinks = [
        passed_along(sets if slot < last else tied(sets, given_sinks[0]), -by)
        for slot, (by, sets) in enumerate(zip(steps, chosen))
    ]

    tau = lax.all_to_all(
        tied(regrouped(perambulator, high, half, pair_count), given_counts, *wanted),
        "tm",
        split_axis=0,
        concat_axis=0,
        axis_index_groups=halves,
        tiled=True,
    ).reshape(half, 2 * pair_count, columns, width)
    if columns % 16 != 0:
        tau = jnp.moveaxis(tau, 1, 0).reshape(2 * pair_count, -1, vectors, width)
        tau = jnp.moveaxis(tau, 0, 1)

    sums = jnp.zeros((2 * pair_count, 2, slots), jnp.float32)
    sums = pairs_sums(tau, 0, 0, given_sinks, given_sources, given_counts, sums)
    sums = pairs_sums(tau, 1, 0, own_sinks[:last], own_sources, counts, sums)
    got = exchanged(sums, half)
    sums = pairs_sums(tau, 1, last, own_sinks[last:], own_sources, counts, sums)
    total = (sums[pair_count:] + got[:pair_count]) / (columns * devices)
    return jnp.swapaxes(total, 1, 2)


def solution(mesh):
    return jax.shard_map(
        body,
        mesh=mesh,
        in_specs=(
            P("groups", "tm", None),
            P(("groups", "tm"), None, None, None),
            P("tm", None, None),
            P("tm"),
        ),
        out_specs=P(("groups", "tm"), None, None),
        check_vma=False,
    )
```

profile of v0, /device:TPU:12, one launch (start us, length us, event | category | flops | bytes accessed | tf_op | source)
XLA Modules:
  0.0 150.9 jit_solution(16256766857888469154)
XLA Ops:
  0.0 0.0 copy-start
  0.0 0.8 slice_bitcast_fusion
  0.8 1.0 collective-permute-start.1
  1.9 0.4 collective-permute-start.2
  2.3 2.6 %collective-permute-start = (s32[2]{0:T(128)}, s32[2]{0:T(128)S(1)}, u32[]{:S(2)}, u32[]{:S(2)}) collective-permute-start(s32[2]{0:T(128)} %counts_ref.3), channel_id=1, source_target_pairs={{0,8},{1,9},{2,10},{3,11},{4,12},{5,13},{6,14},{7,15},{8,0},{9,1},... | collective-permute-start | bytes 32 | tf_op jit(solution)/shard_map/ppermute | solution.py:20
  4.8 4.4 %shard_map.46.refs_0_ = bf16[8,2,2,48,1536]{4,3,2,1,0:T(8,128)(2,1)} custom-call(s32[1]{0:T(128)} %bitcast.high_ref, bf16[2,8,2,48,1536]{4,3,2,1,0:T(8,128)(2,1)} %bitcast.14), custom_call_target="tpu_custom_call" | custom-call | tf_op jit(solution)/shard_map/pallas_call | solution.py:55
  9.2 0.0 collective-permute-done.refs_1_.counts_ref
  9.2 0.0 copy-start.7
  9.3 0.0 collective-permute-done.1.refs_2_
  9.3 0.0 copy-start.4
  9.3 0.0 collective-permute-done.2.refs_3_
  9.3 0.5 copy-done.7
  9.8 0.0 copy-done.4
  9.8 0.0 copy-start.2
  9.8 0.5 copy-done.2
  10.3 0.0 copy-start.6
  10.3 0.0 copy-start.3
  10.3 5.9 %all-to-all-start = ((bf16[8,2,2,48,1536]{4,3,2,1,0:T(8,128)(2,1)}), bf16[8,2,2,48,1536]{4,3,2,1,0:T(8,128)(2,1)}, u32[]{:S(2)}, u32[]{:S(2)}) async-start(bf16[8,2,2,48,1536]{4,3,2,1,0:T(8,128)(2,1)} %shard_map.47), calls=%async_computation | async-start | bytes 9437184 | tf_op jit(solution)/shard_map/all_to_all | solution.py:217
  16.3 0.0 copy-done.6
  16.3 0.1 reshape.40
  16.4 0.0 copy-done
  16.4 1.6 %gather_fusion.2 = bf16[6,192,384]{2,1,0:T(8,128)(2,1)} fusion(bf16[16,192,384]{2,1,0:T(8,128)(2,1)S(1)} %bitcast.13, s32[1024]{0:T(1024)S(1)} %pad_clamp_fusion), kind=kCustom, calls=%fused_computation.2 | custom fusion | bytes 1769496 | tf_op jit(solution)/shard_map/jit(_take)/gather | solution.py:206
  18.0 2.6 %collective-permute-start.5 = (bf16[2,3,192,384]{3,2,1,0:T(8,128)(2,1)}, bf16[2,3,192,384]{3,2,1,0:T(8,128)(2,1)}, u32[]{:S(2)}, u32[]{:S(2)}) collective-permute-start(bf16[2,3,192,384]{3,2,1,0:T(8,128)(2,1)} %bitcast.6.refs_1_), channel_id=1, source_target_pairs={{0,8},{1,9},{2,10},{3,11},{4,12},{5,13},{6,14},{7,15},{8,0},{9,1},... | collective-permute-start | bytes 2654216 | tf_op jit(solution)/shard_map/ppermute | solution.py:20
  20.6 0.0 copy-done.5
  20.6 0.6 gather_fusion
  21.2 0.1 collective-permute-start.3
  21.3 0.0 copy-done.3
  21.3 0.6 gather_fusion.1
  22.0 0.0 copy-start.1
  22.0 1.5 %collective-permute-start.4 = (bf16[3,192,384]{2,1,0:T(8,128)(2,1)S(1)}, bf16[3,192,384]{2,1,0:T(8,128)(2,1)}, u32[]{:S(2)}, u32[]{:S(2)}) collective-permute-start(bf16[3,192,384]{2,1,0:T(8,128)(2,1)S(1)} %gather_fusion.1), channel_id=1, source_target_pairs={{0,14},{1,15},{2,0},{3,1},{4,2},{5,3},{6,4},{7,5},{8,6},{9,7},{10,... | collective-permute-start | bytes 1327112 | tf_op jit(solution)/shard_map/ppermute | solution.py:25
  23.5 3.2 %collective-permute-start.6 = (bf16[3,192,384]{2,1,0:T(8,128)(2,1)S(1)}, bf16[3,192,384]{2,1,0:T(8,128)(2,1)}, u32[]{:S(2)}, u32[]{:S(2)}) collective-permute-start(bf16[3,192,384]{2,1,0:T(8,128)(2,1)S(1)} %gather_fusion), channel_id=1, source_target_pairs={{0,11},{1,12},{2,13},{3,14},{4,15},{5,0},{6,1},{7,2},{8,3},{9,4},{... | collective-permute-start | bytes 1327112 | tf_op jit(solution)/shard_map/ppermute | solution.py:25
  26.7 71.2 %collective-permute-done.3.refs_0_.refs_1_ = bf16[3,192,384]{2,1,0:T(8,128)(2,1)} collective-permute-done((bf16[3,192,384]{2,1,0:T(8,128)(2,1)S(1)}, bf16[3,192,384]{2,1,0:T(8,128)(2,1)}, u32[]{:S(2)}, u32[]{:S(2)}) %collective-permute-start.3) | collective-permute-done | bytes 442400 | tf_op jit(solution)/shard_map/ppermute | solution.py:25
  98.0 0.0 collective-permute-done.4.refs_1_
  98.0 0.0 copy-done.1
  98.0 9.7 %collective-permute-start.7 = (bf16[3,192,384]{2,1,0:T(8,128)(2,1)}, bf16[3,192,384]{2,1,0:T(8,128)(2,1)S(1)}, u32[]{:S(2)}, u32[]{:S(2)}) collective-permute-start(bf16[3,192,384]{2,1,0:T(8,128)(2,1)} %shard_map.50), channel_id=1, source_target_pairs={{0,6},{1,7},{2,8},{3,9},{4,10},{5,11},{6,12},{7,13},{8,14},{9,15},... | collective-permute-start | bytes 1327112 | tf_op jit(solution)/shard_map/ppermute | solution.py:25
  107.7 0.0 collective-permute-done.5.refs_2_
  107.7 0.0 all-to-all-done
  107.7 0.6 broadcast_3_begin_ref.2.begin_ref
  108.3 9.5 %shard_map.48.begin_ref = f32[4,2,3]{2,1,0:T(2,128)} custom-call(s32[2]{0:T(128)} %copy-done.7, f32[4,2,3]{2,1,0:T(2,128)} %broadcast_3_begin_ref.2.begin_ref, bf16[8,4,48,1536]{3,2,1,0:T(8,128)(2,1)} %bitcast.4.tau_ref, bf16[3,192,384]{2,1,0:T(8,128)(2,1)} %collective-permute-done.3.refs_0_.refs_1_, bf16[3,192,384]{2,1,0:T(8,128)(2,1)} %collective-permute-done.4.refs_1_, ...), custom_call_target="tpu_custom_call" | custom-call | flops 5435817984 | bytes 4128768 | tf_op jit(solution)/shard_map/pallas_call | solution.py:169
  117.8 0.0 collective-permute-done.6.refs_0_
  117.8 11.8 %shard_map.49.begin_ref = f32[4,2,3]{2,1,0:T(2,128)} custom-call(s32[2]{0:T(128)} %counts_ref.3, f32[4,2,3]{2,1,0:T(2,128)} %shard_map.48.begin_ref, bf16[8,4,48,1536]{3,2,1,0:T(8,128)(2,1)} %bitcast.4.tau_ref, bf16[3,192,384]{2,1,0:T(8,128)(2,1)} %collective-permute-done.6.refs_0_, bf16[2,3,192,384]{3,2,1,0:T(8,128)(2,1)} %bitcast.6.refs_1_), custom_call_target="tpu_custom_call" | custom-call | flops 2717908992 | bytes 2064384 | tf_op jit(solution)/shard_map/pallas_call | solution.py:169
  129.6 7.3 %collective-permute-start.8 = (f32[4,2,3]{2,1,0:T(2,128)}, f32[4,2,3]{2,1,0:T(2,128)S(1)}, u32[]{:S(2)}, u32[]{:S(2)}) collective-permute-start(f32[4,2,3]{2,1,0:T(2,128)} %shard_map.49.begin_ref), channel_id=1, source_target_pairs={{0,8},{1,9},{2,10},{3,11},{4,12},{5,13},{6,14},{7,15},{8,0},{9,1},... | collective-permute-start | bytes 296 | tf_op jit(solution)/shard_map/ppermute | solution.py:20
  137.0 0.0 collective-permute-done.7.refs_0_
  137.0 0.0 copy-start.8
  137.0 0.8 copy-done.8
  137.8 11.8 %shard_map.51 = f32[4,2,3]{2,1,0:T(2,128)} custom-call(s32[2]{0:T(128)} %counts_ref.3, f32[4,2,3]{2,1,0:T(2,128)} %shard_map.49.begin_ref, bf16[8,4,48,1536]{3,2,1,0:T(8,128)(2,1)} %bitcast.4.tau_ref, bf16[3,192,384]{2,1,0:T(8,128)(2,1)} %copy-done.8, bf16[2,3,192,384]{3,2,1,0:T(8,128)(2,1)} %bitcast.6.refs_1_), custom_call_target="tpu_custom_call" | custom-call | flops 2717908992 | bytes 2064384 | tf_op jit(solution)/shard_map/pallas_call | solution.py:169
  149.6 0.0 collective-permute-done.8
  149.6 1.3 fusion.1
  (7 shorter events, 0.0 us)
Async XLA Ops:
  0.0 16.4 %copy-start = (bf16[1,16,192,384]{3,2,1,0:T(8,128)(2,1)S(1)}, bf16[1,16,192,384]{3,2,1,0:T(8,128)(2,1)}, u32[]{:S(2)}) copy-start(bf16[1,16,192,384]{3,2,1,0:T(8,128)(2,1)} %param.5) | copy-start | bytes 7077892
  0.8 8.4 %collective-permute-start.1 = (s32[3]{0:T(128)S(1)}, s32[3]{0:T(128)S(1)}, u32[]{:S(2)}, u32[]{:S(2)}) collective-permute-start(s32[3]{0:T(128)S(1)} %get-tuple-element.6), channel_id=1, source_target_pairs={{0,5},{1,6},{2,7},{3,8},{4,9},{5,10},{6,11},{7,12},{8,13},{9,14},{... | collective-permute-start | bytes 44 | tf_op jit(solution)/shard_map/ppermute | solution.py:25
  1.9 7.4 %collective-permute-start.2 = (s32[3]{0:T(128)S(1)}, s32[3]{0:T(128)S(1)}, u32[]{:S(2)}, u32[]{:S(2)}) collective-permute-start(s32[3]{0:T(128)S(1)} %get-tuple-element.5), channel_id=1, source_target_pairs={{0,10},{1,11},{2,12},{3,13},{4,14},{5,15},{6,0},{7,1},{8,2},{9,3},... | collective-permute-start | bytes 44 | tf_op jit(solution)/shard_map/ppermute | solution.py:25
  2.3 7.0 %collective-permute-start = (s32[2]{0:T(128)}, s32[2]{0:T(128)S(1)}, u32[]{:S(2)}, u32[]{:S(2)}) collective-permute-start(s32[2]{0:T(128)} %counts_ref.3), channel_id=1, source_target_pairs={{0,8},{1,9},{2,10},{3,11},{4,12},{5,13},{6,14},{7,15},{8,0},{9,1},... | collective-permute-start | bytes 32 | tf_op jit(solution)/shard_map/ppermute | solution.py:20
  9.2 0.5 copy-start.7
  9.3 0.5 copy-start.4
  9.8 0.5 copy-start.2
  10.3 5.9 %copy-start.6 = (s32[2,3,2]{1,2,0:T(2,128)S(1)}, s32[2,3,2]{1,2,0:T(2,128)}, u32[]{:S(2)}) copy-start(s32[2,3,2]{1,2,0:T(2,128)} %param.6) | copy-start | bytes 148
  10.3 10.3 %copy-start.5 = (s32[3]{0:T(128)S(1)}, s32[3]{0:T(128)}, u32[]{:S(2)}) copy-start(s32[3]{0:T(128)} %copy-done.4) | copy-start | bytes 40
  10.3 11.0 %copy-start.3 = (s32[3]{0:T(128)S(1)}, s32[3]{0:T(128)}, u32[]{:S(2)}) copy-start(s32[3]{0:T(128)} %copy-done.2) | copy-start | bytes 40
  10.3 97.4 %all-to-all-start = ((bf16[8,2,2,48,1536]{4,3,2,1,0:T(8,128)(2,1)}), bf16[8,2,2,48,1536]{4,3,2,1,0:T(8,128)(2,1)}, u32[]{:S(2)}, u32[]{:S(2)}) async-start(bf16[8,2,2,48,1536]{4,3,2,1,0:T(8,128)(2,1)} %shard_map.47), calls=%async_computation | async-start | bytes 9437184 | tf_op jit(solution)/shard_map/all_to_all | solution.py:217
  18.0 89.7 %collective-permute-start.5 = (bf16[2,3,192,384]{3,2,1,0:T(8,128)(2,1)}, bf16[2,3,192,384]{3,2,1,0:T(8,128)(2,1)}, u32[]{:S(2)}, u32[]{:S(2)}) collective-permute-start(bf16[2,3,192,384]{3,2,1,0:T(8,128)(2,1)} %bitcast.6.refs_1_), channel_id=1, source_target_pairs={{0,8},{1,9},{2,10},{3,11},{4,12},{5,13},{6,14},{7,15},{8,0},{9,1},... | collective-permute-start | bytes 2654216 | tf_op jit(solution)/shard_map/ppermute | solution.py:20
  21.2 76.7 %collective-permute-start.3 = (bf16[3,192,384]{2,1,0:T(8,128)(2,1)S(1)}, bf16[3,192,384]{2,1,0:T(8,128)(2,1)}, u32[]{:S(2)}, u32[]{:S(2)}) collective-permute-start(bf16[3,192,384]{2,1,0:T(8,128)(2,1)S(1)} %gather_fusion), channel_id=1, source_target_pairs={{0,3},{1,4},{2,5},{3,6},{4,7},{5,8},{6,9},{7,10},{8,11},{9,12},{10... | collective-permute-start | bytes 1327112 | tf_op jit(solution)/shard_map/ppermute | solution.py:25
  22.0 76.0 %copy-start.1 = (bf16[3,192,384]{2,1,0:T(8,128)(2,1)}, bf16[3,192,384]{2,1,0:T(8,128)(2,1)S(1)}, u32[]{:S(2)}) copy-start(bf16[3,192,384]{2,1,0:T(8,128)(2,1)S(1)} %gather_fusion.1) | copy-start | bytes 1327108
  22.0 76.0 %collective-permute-start.4 = (bf16[3,192,384]{2,1,0:T(8,128)(2,1)S(1)}, bf16[3,192,384]{2,1,0:T(8,128)(2,1)}, u32[]{:S(2)}, u32[]{:S(2)}) collective-permute-start(bf16[3,192,384]{2,1,0:T(8,128)(2,1)S(1)} %gather_fusion.1), channel_id=1, source_target_pairs={{0,14},{1,15},{2,0},{3,1},{4,2},{5,3},{6,4},{7,5},{8,6},{9,7},{10,... | collective-permute-start | bytes 1327112 | tf_op jit(solution)/shard_map/ppermute | solution.py:25
  23.5 94.3 %collective-permute-start.6 = (bf16[3,192,384]{2,1,0:T(8,128)(2,1)S(1)}, bf16[3,192,384]{2,1,0:T(8,128)(2,1)}, u32[]{:S(2)}, u32[]{:S(2)}) collective-permute-start(bf16[3,192,384]{2,1,0:T(8,128)(2,1)S(1)} %gather_fusion), channel_id=1, source_target_pairs={{0,11},{1,12},{2,13},{3,14},{4,15},{5,0},{6,1},{7,2},{8,3},{9,4},{... | collective-permute-start | bytes 1327112 | tf_op jit(solution)/shard_map/ppermute | solution.py:25
  98.0 39.0 %collective-permute-start.7 = (bf16[3,192,384]{2,1,0:T(8,128)(2,1)}, bf16[3,192,384]{2,1,0:T(8,128)(2,1)S(1)}, u32[]{:S(2)}, u32[]{:S(2)}) collective-permute-start(bf16[3,192,384]{2,1,0:T(8,128)(2,1)} %shard_map.50), channel_id=1, source_target_pairs={{0,6},{1,7},{2,8},{3,9},{4,10},{5,11},{6,12},{7,13},{8,14},{9,15},... | collective-permute-start | bytes 1327112 | tf_op jit(solution)/shard_map/ppermute | solution.py:25
  129.6 20.0 %collective-permute-start.8 = (f32[4,2,3]{2,1,0:T(2,128)}, f32[4,2,3]{2,1,0:T(2,128)S(1)}, u32[]{:S(2)}, u32[]{:S(2)}) collective-permute-start(f32[4,2,3]{2,1,0:T(2,128)} %shard_map.49.begin_ref), channel_id=1, source_target_pairs={{0,8},{1,9},{2,10},{3,11},{4,12},{5,13},{6,14},{7,15},{8,0},{9,1},... | collective-permute-start | bytes 296 | tf_op jit(solution)/shard_map/ppermute | solution.py:20
  137.0 0.8 copy-start.8
where the time goes:
time: 151 us
  waiting for transfers between devices  71.3 us (47%)
  Pallas kernels  37.5 us (25%)
  starting transfers between devices  34.4 us (23%)
  local copies, waits for them, and re-layouts  6.26 us (4%)
    ppermute x6, waiting for transfers between devices, passed_along(): lax.ppermute(x, 'tm', [(i, (i + by) % devices ^ mask) for i in range(devi...  71.3 us
    pallas_call x3, Pallas kernels, pairs_sums(): pl.pallas_call(functools.partial(pairs_kernel, pairs, lead, first), grid=...  33.2 us
    ppermute x6, starting transfers between devices, passed_along(): lax.ppermute(x, 'tm', [(i, (i + by) % devices ^ mask) for i in range(devi...  15.9 us
    ppermute x3, starting transfers between devices, exchanged(): return lax.ppermute(x, 'tm', [(i, i ^ mask) for i in range(devices)])  12.5 us
    all_to_all x1, starting transfers between devices, body(): lax.all_to_all(tied(regrouped(perambulator, high, half, pair_count), give...  5.94 us
    pallas_call x1, Pallas kernels, regrouped(): pl.pallas_call(regroup_kernel, in_specs=[SMEM, HBM], out_specs=HBM, out_s...  4.37 us
  transfers between devices with their start and end apart: 10, of which 1 were waited for; matrix products, arithmetic and copies ran while one was open for 2% of the time, Pallas kernels for 25%

commit v1 on v0

--- a/solution.py
+++ b/solution.py
@@ -81,9 +81,13 @@
     return jnp.concatenate([x[:, vectors:], x[:, :vectors]], axis=1)
 
 
-def pairs_kernel(pairs, lead, first, counts_ref, begin_ref, tau_ref, *refs):
+def pairs_kernel(pairs, lead, first, begins, counts_ref, tau_ref, *refs):
+    begin_ref = refs[0] if begins else None
+    refs = refs[begins:]
     sink_refs = refs[:pairs]
-    source_ref, out_ref, sinks, sources, both_ref, left_ref, sink_sems, source_sems = refs[pairs:]
+    source_ref, out_ref, sinks, sources, tall_ref, turned_ref, left_ref, sink_sems, source_sems = (
+        refs[pairs:]
+    )
     slots, vectors, packed = sinks.shape[1:]
     spins, _, width = left_ref.shape
     blocks = width // packed
@@ -108,15 +112,19 @@
         for p in range(out_ref.shape[0]):
             for d in range(slots):
                 for side in range(2):
-                    out_ref[p, side, d] = begin_ref[p, side, d]
+                    out_ref[p, side, d] = begin_ref[p, side, d] if begins else 0.0
+
+    def part(s, b):
+        lanes = slice(b * packed, (b + 1) * packed)
+        return tau_ref[s * pieces : (s + 1) * pieces, 0, :, lanes].reshape(vectors, packed)
 
     for s in range(spins):
         for b in range(blocks):
-            lanes = slice(b * packed, (b + 1) * packed)
-            tile = tau_ref[s * pieces : (s + 1) * pieces, 0, :, lanes].reshape(vectors, packed)
-            swapped = halves_swapped(tile)
-            both_ref[s, :vectors, lanes] = tile
-            both_ref[s, vectors:, lanes] = jnp.where(first_half, -swapped, swapped)
+            tall = part(s, b).T
+            middle = b * packed + vectors
+            tall_ref[s, b * packed : (b + 1) * packed] = tall
+            turned_ref[s, b * packed : middle] = -tall[vectors:]
+            turned_ref[s, middle : (b + 1) * packed] = tall[:vectors]
 
     @pl.loop(0, counts_ref[first + pair])
     def _(d):
@@ -128,10 +136,7 @@
             [jnp.where(first_half, sink, -sink), halves_swapped(sink)], axis=0
         )
         for s in range(spins):
-            stacked = jnp.concatenate(
-                [both_ref[s, :vectors, b * packed : (b + 1) * packed] for b in range(blocks)],
-                axis=0,
-            )
+            stacked = jnp.concatenate([part(s, b) for b in range(blocks)], axis=0)
             left = lax.dot_general(
                 stacked, embedding, NT_DIMS, preferred_element_type=jnp.float32
             ).astype(jnp.bfloat16)
@@ -139,25 +144,23 @@
                 left_ref[s, :, b * packed : (b + 1) * packed] = left[
                     b * vectors : (b + 1) * vectors
                 ]
-        block = jnp.zeros((2 * vectors, vectors), jnp.float32)
+        block_real = jnp.zeros((vectors, vectors), jnp.float32)
+        block_imag = jnp.zeros((vectors, vectors), jnp.float32)
         for s in range(spins):
-            block += lax.dot_general(
-                both_ref[s], left_ref[s], NT_DIMS, preferred_element_type=jnp.float32
-            )
+            block_real += jnp.dot(left_ref[s], tall_ref[s], preferred_element_type=jnp.float32)
+            block_imag += jnp.dot(left_ref[s], turned_ref[s], preferred_element_type=jnp.float32)
         pltpu.make_async_copy(
             source_ref.at[0, 0], sources.at[pair, d], source_sems.at[pair, d]
         ).wait()
-        source = sources[pair, d].astype(jnp.float32).T
-        real = source[:vectors]
-        imag = source[vectors:]
-        block_real = block[:vectors]
-        block_imag = block[vectors:]
+        source = sources[pair, d].astype(jnp.float32)
+        real = source[:, :vectors]
+        imag = source[:, vectors:]
         row = lead + first + pair
         out_ref[row, 0, d] += jnp.sum(real * block_real - imag * block_imag)
         out_ref[row, 1, d] += jnp.sum(real * block_imag + imag * block_real)
 
 
-def pairs_sums(tau, side, first, sinks, sources, counts, begin):
+def pairs_sums(tau, side, first, sinks, sources, counts, *begin):
     pairs = len(sinks)
     slots, vectors, packed = sinks[0].shape
     pieces, _, columns, width = tau.shape
@@ -167,26 +170,27 @@
     moved = 2 * pairs * (spins * vectors * width + 2 * slots * vectors * packed)
     elemental_copies = [pltpu.VMEM((pairs, slots, vectors, packed), jnp.bfloat16)] * 2
     return pl.pallas_call(
-        functools.partial(pairs_kernel, pairs, lead, first),
+        functools.partial(pairs_kernel, pairs, lead, first, len(begin)),
         grid=(pairs,),
         in_specs=[
             SMEM,
-            SMEM,
             pl.BlockSpec((pieces, 1, columns, width), lambda p: (0, lead + first + p, 0, 0)),
         ]
+        + [SMEM] * len(begin)
         + [HBM] * (pairs + 1),
         out_specs=SMEM,
-        out_shape=jax.ShapeDtypeStruct(begin.shape, jnp.float32),
+        out_shape=jax.ShapeDtypeStruct((2 * counts.shape[0], 2, slots), jnp.float32),
         scratch_shapes=elemental_copies
         + [
-            pltpu.VMEM((spins, 2 * vectors, width), jnp.bfloat16),
+            pltpu.VMEM((spins, width, vectors), jnp.bfloat16),
+            pltpu.VMEM((spins, width, vectors), jnp.bfloat16),
             pltpu.VMEM((spins, vectors, width), jnp.bfloat16),
             pltpu.SemaphoreType.DMA((pairs, slots)),
             pltpu.SemaphoreType.DMA((pairs, slots)),
         ],
         compiler_params=pltpu.CompilerParams(vmem_limit_bytes=VMEM_BYTES),
         cost_estimate=pl.CostEstimate(flops=flops, bytes_accessed=moved, transcendentals=0),
-    )(counts, begin, tau, *sinks, sources)
+    )(counts, tau, *begin, *sinks, sources)
 
 
 def body(perambulator, elementals, diagrams, counts):
@@ -226,8 +230,7 @@
         tau = jnp.moveaxis(tau, 1, 0).reshape(2 * pair_count, -1, vectors, width)
         tau = jnp.moveaxis(tau, 0, 1)
 
-    sums = jnp.zeros((2 * pair_count, 2, slots), jnp.float32)
-    sums = pairs_sums(tau, 0, 0, given_sinks, given_sources, given_counts, sums)
+    sums = pairs_sums(tau, 0, 0, given_sinks, given_sources, given_counts)
     sums = pairs_sums(tau, 1, 0, own_sinks[:last], own_sources, counts, sums)
     got = exchanged(sums, half)
     sums = pairs_sums(tau, 1, last, own_sinks[last:], own_sources, counts, sums)

time: 151 us -> 145 us (0.960)
  the two profiles are of different devices: /device:TPU:12 before, /device:TPU:1 now
where the time goes in v1:
time: 145 us
  waiting for transfers between devices  82.8 us (57%)
  Pallas kernels  29.4 us (20%)
  starting transfers between devices  25.7 us (18%)
  local copies, waits for them, and re-layouts  5.67 us (4%)
    ppermute x6, waiting for transfers between devices, passed_along(): lax.ppermute(x, 'tm', [(i, (i + by) % devices ^ mask) for i in range(devi...  82.8 us
    pallas_call x3, Pallas kernels, pairs_sums(): pl.pallas_call(functools.partial(pairs_kernel, pairs, lead, first, len(be...  25.1 us
    ppermute x3, starting transfers between devices, exchanged(): return lax.ppermute(x, 'tm', [(i, i ^ mask) for i in range(devices)])  11.9 us
    ppermute x6, starting transfers between devices, passed_along(): lax.ppermute(x, 'tm', [(i, (i + by) % devices ^ mask) for i in range(devi...  9.11 us
    all_to_all x1, starting transfers between devices, body(): lax.all_to_all(tied(regrouped(perambulator, high, half, pair_count), give...  4.69 us
    pallas_call x1, Pallas kernels, regrouped(): pl.pallas_call(regroup_kernel, in_specs=[SMEM, HBM], out_specs=HBM, out_s...  4.37 us
  transfers between devices with their start and end apart: 10, of which 3 were waited for; matrix products, arithmetic and copies ran while one was open for 2% of the time, Pallas kernels for 20%

profile of v1, /device:TPU:1, one launch (start us, length us, event | category | flops | bytes accessed | tf_op | source)
XLA Modules:
  0.0 145.1 jit_solution(5939287607100024682)
XLA Ops:
  0.0 0.0 copy-start
  0.0 0.8 slice_bitcast_fusion
  0.8 3.6 %collective-permute-start.1 = (s32[3]{0:T(128)S(1)}, s32[3]{0:T(128)S(1)}, u32[]{:S(2)}, u32[]{:S(2)}) collective-permute-start(s32[3]{0:T(128)S(1)} %get-tuple-element.6), channel_id=1, source_target_pairs={{0,5},{1,6},{2,7},{3,8},{4,9},{5,10},{6,11},{7,12},{8,13},{9,14},{... | collective-permute-start | bytes 44 | tf_op jit(solution)/shard_map/ppermute | solution.py:25
  4.5 0.5 collective-permute-start.2
  4.9 2.9 %collective-permute-start = (s32[2]{0:T(128)}, s32[2]{0:T(128)S(1)}, u32[]{:S(2)}, u32[]{:S(2)}) collective-permute-start(s32[2]{0:T(128)} %counts_ref.3), channel_id=1, source_target_pairs={{0,8},{1,9},{2,10},{3,11},{4,12},{5,13},{6,14},{7,15},{8,0},{9,1},... | collective-permute-start | bytes 32 | tf_op jit(solution)/shard_map/ppermute | solution.py:20
  7.8 4.4 %shard_map.46.refs_0_ = bf16[8,2,2,48,1536]{4,3,2,1,0:T(8,128)(2,1)} custom-call(s32[1]{0:T(128)} %bitcast.high_ref, bf16[2,8,2,48,1536]{4,3,2,1,0:T(8,128)(2,1)} %bitcast.14), custom_call_target="tpu_custom_call" | custom-call | tf_op jit(solution)/shard_map/pallas_call | solution.py:55
  12.2 0.0 collective-permute-done.refs_1_.counts_ref
  12.2 0.0 copy-start.7
  12.2 0.0 collective-permute-done.1.refs_2_
  12.2 0.0 copy-start.4
  12.2 0.0 collective-permute-done.2.refs_3_
  12.2 0.5 copy-done.7
  12.7 0.0 copy-done.4
  12.7 0.0 copy-start.2
  12.7 0.5 copy-done.2
  13.3 0.0 copy-start.6
  13.3 0.0 copy-start.5
  13.3 0.0 copy-start.3
  13.3 4.7 %all-to-all-start = ((bf16[8,2,2,48,1536]{4,3,2,1,0:T(8,128)(2,1)}), bf16[8,2,2,48,1536]{4,3,2,1,0:T(8,128)(2,1)}, u32[]{:S(2)}, u32[]{:S(2)}) async-start(bf16[8,2,2,48,1536]{4,3,2,1,0:T(8,128)(2,1)} %shard_map.47), calls=%async_computation | async-start | bytes 9437184 | tf_op jit(solution)/shard_map/all_to_all | solution.py:221
  18.0 0.0 copy-done.6
  18.0 0.1 reshape.40
  18.1 0.0 copy-done
  18.1 1.6 %gather_fusion.2 = bf16[6,192,384]{2,1,0:T(8,128)(2,1)} fusion(bf16[16,192,384]{2,1,0:T(8,128)(2,1)S(1)} %bitcast.13, s32[1024]{0:T(1024)S(1)} %pad_clamp_fusion), kind=kCustom, calls=%fused_computation.2 | custom fusion | bytes 1769496 | tf_op jit(solution)/shard_map/jit(_take)/gather | solution.py:210
  19.7 1.7 %collective-permute-start.5 = (bf16[2,3,192,384]{3,2,1,0:T(8,128)(2,1)}, bf16[2,3,192,384]{3,2,1,0:T(8,128)(2,1)}, u32[]{:S(2)}, u32[]{:S(2)}) collective-permute-start(bf16[2,3,192,384]{3,2,1,0:T(8,128)(2,1)} %bitcast.6.refs_2_), channel_id=1, source_target_pairs={{0,8},{1,9},{2,10},{3,11},{4,12},{5,13},{6,14},{7,15},{8,0},{9,1},... | collective-permute-start | bytes 2654216 | tf_op jit(solution)/shard_map/ppermute | solution.py:20
  21.4 0.0 copy-done.5
  21.4 0.6 gather_fusion
  22.0 2.0 %collective-permute-start.3 = (bf16[3,192,384]{2,1,0:T(8,128)(2,1)S(1)}, bf16[3,192,384]{2,1,0:T(8,128)(2,1)}, u32[]{:S(2)}, u32[]{:S(2)}) collective-permute-start(bf16[3,192,384]{2,1,0:T(8,128)(2,1)S(1)} %gather_fusion), channel_id=1, source_target_pairs={{0,3},{1,4},{2,5},{3,6},{4,7},{5,8},{6,9},{7,10},{8,11},{9,12},{10... | collective-permute-start | bytes 1327112 | tf_op jit(solution)/shard_map/ppermute | solution.py:25
  24.0 0.0 copy-done.3
  24.0 0.6 gather_fusion.1
  24.7 0.0 copy-start.1
  24.7 3.0 %collective-permute-start.4 = (bf16[3,192,384]{2,1,0:T(8,128)(2,1)S(1)}, bf16[3,192,384]{2,1,0:T(8,128)(2,1)}, u32[]{:S(2)}, u32[]{:S(2)}) collective-permute-start(bf16[3,192,384]{2,1,0:T(8,128)(2,1)S(1)} %gather_fusion.1), channel_id=1, source_target_pairs={{0,14},{1,15},{2,0},{3,1},{4,2},{5,3},{6,4},{7,5},{8,6},{9,7},{10,... | collective-permute-start | bytes 1327112 | tf_op jit(solution)/shard_map/ppermute | solution.py:25
  27.7 0.0 collective-permute-start.6
  27.7 76.0 %collective-permute-done.3.refs_0_.refs_1_ = bf16[3,192,384]{2,1,0:T(8,128)(2,1)} collective-permute-done((bf16[3,192,384]{2,1,0:T(8,128)(2,1)S(1)}, bf16[3,192,384]{2,1,0:T(8,128)(2,1)}, u32[]{:S(2)}, u32[]{:S(2)}) %collective-permute-start.3) | collective-permute-done | bytes 442400 | tf_op jit(solution)/shard_map/ppermute | solution.py:25
  103.8 5.2 %collective-permute-done.4.refs_1_ = bf16[3,192,384]{2,1,0:T(8,128)(2,1)} collective-permute-done((bf16[3,192,384]{2,1,0:T(8,128)(2,1)S(1)}, bf16[3,192,384]{2,1,0:T(8,128)(2,1)}, u32[]{:S(2)}, u32[]{:S(2)}) %collective-permute-start.4) | collective-permute-done | bytes 442400 | tf_op jit(solution)/shard_map/ppermute | solution.py:25
  108.9 0.0 copy-done.1
  108.9 0.0 collective-permute-start.7
  108.9 0.0 collective-permute-done.5.refs_2_
  108.9 0.0 all-to-all-done
  108.9 7.5 %shard_map.48.refs_0_ = f32[4,2,3]{2,1,0:T(2,128)} custom-call(s32[2]{0:T(128)} %copy-done.7, bf16[8,4,48,1536]{3,2,1,0:T(8,128)(2,1)} %bitcast.4.tau_ref, bf16[3,192,384]{2,1,0:T(8,128)(2,1)} %collective-permute-done.3.refs_0_.refs_1_, bf16[3,192,384]{2,1,0:T(8,128)(2,1)} %collective-permute-done.4.refs_1_, ...), custom_call_target="tpu_custom_call" | custom-call | flops 5435817984 | bytes 4128768 | tf_op jit(solution)/shard_map/pallas_call | solution.py:172
  116.5 1.6 %collective-permute-done.6.refs_1_ = bf16[3,192,384]{2,1,0:T(8,128)(2,1)} collective-permute-done((bf16[3,192,384]{2,1,0:T(8,128)(2,1)S(1)}, bf16[3,192,384]{2,1,0:T(8,128)(2,1)}, u32[]{:S(2)}, u32[]{:S(2)}) %collective-permute-start.6) | collective-permute-done | bytes 442400 | tf_op jit(solution)/shard_map/ppermute | solution.py:25
  118.1 8.8 %shard_map.49.refs_0_ = f32[4,2,3]{2,1,0:T(2,128)} custom-call(s32[2]{0:T(128)} %counts_ref.3, bf16[8,4,48,1536]{3,2,1,0:T(8,128)(2,1)} %bitcast.4.tau_ref, f32[4,2,3]{2,1,0:T(2,128)} %shard_map.48.refs_0_, bf16[3,192,384]{2,1,0:T(8,128)(2,1)} %collective-permute-done.6.refs_1_, bf16[2,3,192,384]{3,2,1,0:T(8,128)(2,1)} %bitcast.6.refs_2_), custom_call_target="tpu_custom_call" | custom-call | flops 2717908992 | bytes 2064384 | tf_op jit(solution)/shard_map/pallas_call | solution.py:172
  126.9 7.4 %collective-permute-start.8 = (f32[4,2,3]{2,1,0:T(2,128)}, f32[4,2,3]{2,1,0:T(2,128)S(1)}, u32[]{:S(2)}, u32[]{:S(2)}) collective-permute-start(f32[4,2,3]{2,1,0:T(2,128)} %shard_map.49.refs_0_), channel_id=1, source_target_pairs={{0,8},{1,9},{2,10},{3,11},{4,12},{5,13},{6,14},{7,15},{8,0},{9,1},... | collective-permute-start | bytes 296 | tf_op jit(solution)/shard_map/ppermute | solution.py:20
  134.3 0.0 collective-permute-done.7.refs_1_
  134.3 0.0 copy-start.8
  134.3 0.8 copy-done.8
  135.0 8.8 %shard_map.51 = f32[4,2,3]{2,1,0:T(2,128)} custom-call(s32[2]{0:T(128)} %counts_ref.3, bf16[8,4,48,1536]{3,2,1,0:T(8,128)(2,1)} %bitcast.4.tau_ref, f32[4,2,3]{2,1,0:T(2,128)} %shard_map.49.refs_0_, bf16[3,192,384]{2,1,0:T(8,128)(2,1)} %copy-done.8, bf16[2,3,192,384]{3,2,1,0:T(8,128)(2,1)} %bitcast.6.refs_2_), custom_call_target="tpu_custom_call" | custom-call | flops 2717908992 | bytes 2064384 | tf_op jit(solution)/shard_map/pallas_call | solution.py:172
  143.8 0.0 collective-permute-done.8
  143.8 1.3 fusion.1
  (6 shorter events, 0.0 us)
Async XLA Ops:
  0.0 18.1 %copy-start = (bf16[1,16,192,384]{3,2,1,0:T(8,128)(2,1)S(1)}, bf16[1,16,192,384]{3,2,1,0:T(8,128)(2,1)}, u32[]{:S(2)}) copy-start(bf16[1,16,192,384]{3,2,1,0:T(8,128)(2,1)} %param.5) | copy-start | bytes 7077892
  0.8 11.4 %collective-permute-start.1 = (s32[3]{0:T(128)S(1)}, s32[3]{0:T(128)S(1)}, u32[]{:S(2)}, u32[]{:S(2)}) collective-permute-start(s32[3]{0:T(128)S(1)} %get-tuple-element.6), channel_id=1, source_target_pairs={{0,5},{1,6},{2,7},{3,8},{4,9},{5,10},{6,11},{7,12},{8,13},{9,14},{... | collective-permute-start | bytes 44 | tf_op jit(solution)/shard_map/ppermute | solution.py:25
  4.5 7.7 %collective-permute-start.2 = (s32[3]{0:T(128)S(1)}, s32[3]{0:T(128)S(1)}, u32[]{:S(2)}, u32[]{:S(2)}) collective-permute-start(s32[3]{0:T(128)S(1)} %get-tuple-element.5), channel_id=1, source_target_pairs={{0,10},{1,11},{2,12},{3,13},{4,14},{5,15},{6,0},{7,1},{8,2},{9,3},... | collective-permute-start | bytes 44 | tf_op jit(solution)/shard_map/ppermute | solution.py:25
  4.9 7.2 %collective-permute-start = (s32[2]{0:T(128)}, s32[2]{0:T(128)S(1)}, u32[]{:S(2)}, u32[]{:S(2)}) collective-permute-start(s32[2]{0:T(128)} %counts_ref.3), channel_id=1, source_target_pairs={{0,8},{1,9},{2,10},{3,11},{4,12},{5,13},{6,14},{7,15},{8,0},{9,1},... | collective-permute-start | bytes 32 | tf_op jit(solution)/shard_map/ppermute | solution.py:20
  12.2 0.5 copy-start.7
  12.2 0.5 copy-start.4
  12.7 0.5 copy-start.2
  13.3 4.7 %copy-start.6 = (s32[2,3,2]{1,2,0:T(2,128)S(1)}, s32[2,3,2]{1,2,0:T(2,128)}, u32[]{:S(2)}) copy-start(s32[2,3,2]{1,2,0:T(2,128)} %param.6) | copy-start | bytes 148
  13.3 8.1 %copy-start.5 = (s32[3]{0:T(128)S(1)}, s32[3]{0:T(128)}, u32[]{:S(2)}) copy-start(s32[3]{0:T(128)} %copy-done.4) | copy-start | bytes 40
  13.3 10.7 %copy-start.3 = (s32[3]{0:T(128)S(1)}, s32[3]{0:T(128)}, u32[]{:S(2)}) copy-start(s32[3]{0:T(128)} %copy-done.2) | copy-start | bytes 40
  13.3 95.7 %all-to-all-start = ((bf16[8,2,2,48,1536]{4,3,2,1,0:T(8,128)(2,1)}), bf16[8,2,2,48,1536]{4,3,2,1,0:T(8,128)(2,1)}, u32[]{:S(2)}, u32[]{:S(2)}) async-start(bf16[8,2,2,48,1536]{4,3,2,1,0:T(8,128)(2,1)} %shard_map.47), calls=%async_computation | async-start | bytes 9437184 | tf_op jit(solution)/shard_map/all_to_all | solution.py:221
  19.7 89.2 %collective-permute-start.5 = (bf16[2,3,192,384]{3,2,1,0:T(8,128)(2,1)}, bf16[2,3,192,384]{3,2,1,0:T(8,128)(2,1)}, u32[]{:S(2)}, u32[]{:S(2)}) collective-permute-start(bf16[2,3,192,384]{3,2,1,0:T(8,128)(2,1)} %bitcast.6.refs_2_), channel_id=1, source_target_pairs={{0,8},{1,9},{2,10},{3,11},{4,12},{5,13},{6,14},{7,15},{8,0},{9,1},... | collective-permute-start | bytes 2654216 | tf_op jit(solution)/shard_map/ppermute | solution.py:20
  22.0 81.7 %collective-permute-start.3 = (bf16[3,192,384]{2,1,0:T(8,128)(2,1)S(1)}, bf16[3,192,384]{2,1,0:T(8,128)(2,1)}, u32[]{:S(2)}, u32[]{:S(2)}) collective-permute-start(bf16[3,192,384]{2,1,0:T(8,128)(2,1)S(1)} %gather_fusion), channel_id=1, source_target_pairs={{0,3},{1,4},{2,5},{3,6},{4,7},{5,8},{6,9},{7,10},{8,11},{9,12},{10... | collective-permute-start | bytes 1327112 | tf_op jit(solution)/shard_map/ppermute | solution.py:25
  24.7 84.2 %copy-start.1 = (bf16[3,192,384]{2,1,0:T(8,128)(2,1)}, bf16[3,192,384]{2,1,0:T(8,128)(2,1)S(1)}, u32[]{:S(2)}) copy-start(bf16[3,192,384]{2,1,0:T(8,128)(2,1)S(1)} %gather_fusion.1) | copy-start | bytes 1327108
  24.7 84.2 %collective-permute-start.4 = (bf16[3,192,384]{2,1,0:T(8,128)(2,1)S(1)}, bf16[3,192,384]{2,1,0:T(8,128)(2,1)}, u32[]{:S(2)}, u32[]{:S(2)}) collective-permute-start(bf16[3,192,384]{2,1,0:T(8,128)(2,1)S(1)} %gather_fusion.1), channel_id=1, source_target_pairs={{0,14},{1,15},{2,0},{3,1},{4,2},{5,3},{6,4},{7,5},{8,6},{9,7},{10,... | collective-permute-start | bytes 1327112 | tf_op jit(solution)/shard_map/ppermute | solution.py:25
  27.7 90.4 %collective-permute-start.6 = (bf16[3,192,384]{2,1,0:T(8,128)(2,1)S(1)}, bf16[3,192,384]{2,1,0:T(8,128)(2,1)}, u32[]{:S(2)}, u32[]{:S(2)}) collective-permute-start(bf16[3,192,384]{2,1,0:T(8,128)(2,1)S(1)} %gather_fusion), channel_id=1, source_target_pairs={{0,11},{1,12},{2,13},{3,14},{4,15},{5,0},{6,1},{7,2},{8,3},{9,4},{... | collective-permute-start | bytes 1327112 | tf_op jit(solution)/shard_map/ppermute | solution.py:25
  108.9 25.3 %collective-permute-start.7 = (bf16[3,192,384]{2,1,0:T(8,128)(2,1)}, bf16[3,192,384]{2,1,0:T(8,128)(2,1)S(1)}, u32[]{:S(2)}, u32[]{:S(2)}) collective-permute-start(bf16[3,192,384]{2,1,0:T(8,128)(2,1)} %shard_map.50), channel_id=1, source_target_pairs={{0,6},{1,7},{2,8},{3,9},{4,10},{5,11},{6,12},{7,13},{8,14},{9,15},... | collective-permute-start | bytes 1327112 | tf_op jit(solution)/shard_map/ppermute | solution.py:25
  126.9 17.0 %collective-permute-start.8 = (f32[4,2,3]{2,1,0:T(2,128)}, f32[4,2,3]{2,1,0:T(2,128)S(1)}, u32[]{:S(2)}, u32[]{:S(2)}) collective-permute-start(f32[4,2,3]{2,1,0:T(2,128)} %shard_map.49.refs_0_), channel_id=1, source_target_pairs={{0,8},{1,9},{2,10},{3,11},{4,12},{5,13},{6,14},{7,15},{8,0},{9,1},... | collective-permute-start | bytes 296 | tf_op jit(solution)/shard_map/ppermute | solution.py:20
  134.3 0.8 copy-start.8
